TPU v7x, 32 devices: a whole 2x2x4 slice. The times are simulated.
32 devices in a mesh: dp: 8 (over z, y), tensor: 4 (over x, core).
Axes of the slice: x: 2, y: 2, z: 4, core: 2. Of those that a mesh axis runs over, the one named last changes fastest.
Arguments:
- layer_input: bfloat16 [10240, 768], P(('dp', 'tensor')), may hold values from -6 to 6
- cotangent: bfloat16 [10240, 768], P(('dp', 'tensor')), may hold values from -6 to 6
- segments: int32 [10240], replicated, may hold values from 0 to 25, as said below
- parents: int32 [26], replicated, may hold values from 0 to 17, as said below
- norm1_gain: bfloat16 [768], P('dp'), may hold values from 0.099609375 to 1.8984375
- w_query: bfloat16 [768, 768], P('dp', 'tensor'), may hold values from -0.21875 to 0.21875
- w_key: bfloat16 [768, 768], P('dp', 'tensor'), may hold values from -0.21875 to 0.21875
- w_value: bfloat16 [768, 768], P('dp', 'tensor'), may hold values from -0.21875 to 0.21875
- w_out: bfloat16 [768, 768], P('tensor', 'dp'), may hold values from -1.75 to 1.75
- norm2_gain: bfloat16 [768], P('dp'), may hold values from 0.099609375 to 1.8984375
- w_up: bfloat16 [768, 3072], P('dp', 'tensor'), may hold values from -0.21875 to 0.21875
- w_down: bfloat16 [3072, 768], P('tensor', 'dp'), may hold values from -0.109375 to 0.109375
Outputs:
- layer_output: bfloat16 [10240, 768], P(('dp', 'tensor'))
- input_grad: bfloat16 [10240, 768], P(('dp', 'tensor'))
- grad_norm1_gain: float32 [768], P('dp')
- grad_query: float32 [768, 768], P('dp', 'tensor')
- grad_key: float32 [768, 768], P('dp', 'tensor')
- grad_value: float32 [768, 768], P('dp', 'tensor')
- grad_out: float32 [768, 768], P('tensor', 'dp')
- grad_norm2_gain: float32 [768], P('dp')
- grad_up: float32 [768, 3072], P('dp', 'tensor')
- grad_down: float32 [3072, 768], P('tensor', 'dp')
Inputs may be any that keep to these rules, and one draw needn't show every extreme that they name: Tree t holds bytes 5120 t to 5120 (t + 1) - 1 of the stream (the last tree may end at 10240). Its first 2048 bytes are segment 13 t, the trunk; the rest are twelve runs of 256 bytes with the segments 13 t + 1 to 13 t + 12 in some order, every run after the run of its parent segment. parents[s] is the parent segment of s: the trunk 13 t is its own parent, the branches 13 t + 1 to 13 t + 4 have the trunk, and the leaves 13 t + 5 to 13 t + 12 have one of the four branches each, two leaves a branch.
All inputs are finite; a program needn't handle non-finite values.
Results may differ from a plain program's by a relative error of at most 0.017.
Values may be sent and summed in bfloat16 or wider, within the bound.
A program may use at most 256 MiB of HBM per device.

v0:
```python
import math
import jax
import jax.numpy as jnp
from jax import lax
from jax.sharding import PartitionSpec as P

HD = 64
WINDOW = 1536
epsilon = 1e-06
masked_score = -1e30


def from_behind(block, axis, distance):
    devices = range(lax.axis_size(axis))
    route = [(i - distance, i) for i in devices if i - distance in devices]
    return lax.ppermute(block, axis, route)


def split_up(x, dim, peers):
    dims = x.shape
    tiles = x.reshape(*dims[:dim], peers, dims[dim] // peers, *dims[dim + 1 :])
    return jnp.moveaxis(tiles, dim, 0)


def sum_at_owner(x, axis, dim):
    tiles = split_up(x, dim, lax.axis_size(axis))
    arrived = lax.all_to_all(tiles, axis, split_axis=0, concat_axis=0, tiled=True)
    return arrived.astype(jnp.float32).sum(axis=0)


def side_by_side(arrays, axis, dim, along):
    widths = [math.prod(a.shape[along:]) for a in arrays]
    both = jnp.concatenate(
        [a.reshape(*a.shape[:along], w) for a, w in zip(arrays, widths)], axis=along
    )
    whole = sum_at_owner(both, axis, dim)
    tiles = jnp.split(whole, [sum(widths[:k]) for k in range(1, len(widths))], axis=along)
    return tuple((b.reshape(*whole.shape[:along], *a.shape[along:]) for a, b in zip(arrays, tiles)))


def gelu_exact(values):
    return jax.nn.gelu(values, approximate=False)


def row_scale(values):
    return lax.rsqrt(jnp.mean(values * values, axis=-1, keepdims=True) + epsilon)


def norm_backward(incoming, normal_hat, row_factor, gain):
    scaled = incoming * gain
    inner = jnp.mean(scaled * normal_hat, axis=-1, keepdims=True)
    return (row_factor * (scaled - normal_hat * inner), jnp.sum(incoming * normal_hat, axis=0))


def parent_of(seg_ids, parents):
    seg_table = jnp.arange(parents.shape[0], dtype=jnp.int32)
    hits = seg_ids[:, None] == seg_table[None, :]
    return jnp.sum(jnp.where(hits, parents[None, :], 0), axis=1)


def shards(
    layer_input,
    cotangent,
    segments,
    parents,
    norm1_gain,
    w_query,
    w_key,
    w_value,
    w_out,
    norm2_gain,
    w_up,
    w_down,
):
    gain_one, full_query, full_key, full_value, full_out, gain_two, full_up, full_down = (
        lax.all_gather(norm1_gain, "dp", axis=0, tiled=True),
        lax.all_gather(w_query, "dp", axis=0, tiled=True),
        lax.all_gather(w_key, "dp", axis=0, tiled=True),
        lax.all_gather(w_value, "dp", axis=0, tiled=True),
        lax.all_gather(w_out, "dp", axis=1, tiled=True),
        lax.all_gather(norm2_gain, "dp", axis=0, tiled=True),
        lax.all_gather(w_up, "dp", axis=0, tiled=True),
        lax.all_gather(w_down, "dp", axis=1, tiled=True),
    )
    gain_one = gain_one.astype(jnp.float32)
    gain_two = gain_two.astype(jnp.float32)
    row_count = layer_input.shape[0]
    token_count = row_count * lax.axis_size("tensor")
    position = lax.axis_index("dp") * token_count
    head_width = full_query.shape[1]
    head_count = head_width // HD
    scaling = HD ** (-0.5)
    block_rows = min(640, token_count)
    block_count = token_count // block_rows
    span = WINDOW + block_rows
    hop_count = (WINDOW + token_count - 1) // token_count
    inputs = layer_input.astype(jnp.float32)
    factor_one = row_scale(inputs)
    hat_one = inputs * factor_one
    normed = (hat_one * gain_one).astype(jnp.bfloat16)
    normed_all = lax.all_gather(normed, "tensor", axis=0, tiled=True)
    queries = jnp.dot(normed_all, full_query, preferred_element_type=jnp.float32).astype(
        jnp.bfloat16
    )
    keys_own = jnp.dot(normed_all, full_key, preferred_element_type=jnp.float32).astype(
        jnp.bfloat16
    )
    values_own = jnp.dot(normed_all, full_value, preferred_element_type=jnp.float32).astype(
        jnp.bfloat16
    )
    pair_own = jnp.concatenate([keys_own, values_own], axis=1)
    halo_parts = []
    for distance in range(1, hop_count + 1):
        length = min(token_count, WINDOW - (distance - 1) * token_count)
        piece = pair_own[token_count - length :]
        moved = from_behind(piece, "dp", distance)
        halo_parts.append(moved)
    pair_all = jnp.concatenate(halo_parts[::-1] + [pair_own], axis=0)
    seg_padded = jnp.concatenate([jnp.full((WINDOW,), -1, jnp.int32), segments])
    seg_keys = lax.dynamic_slice_in_dim(seg_padded, position, WINDOW + token_count, 0)
    seg_query = seg_keys[WINDOW:]
    parent_one = parent_of(seg_query, parents)
    parent_two = parent_of(parent_one, parents)
    query_spots = jnp.arange(block_rows, dtype=jnp.int32)
    key_spots = jnp.arange(span, dtype=jnp.int32)

    def scores_of(offset):
        query_block = lax.dynamic_slice_in_dim(queries, offset, block_rows, 0).reshape(
            block_rows, head_count, HD
        )
        pair_block = lax.dynamic_slice_in_dim(pair_all, offset, span, 0)
        key_block = pair_block[:, :head_width].reshape(span, head_count, HD)
        value_block = pair_block[:, head_width:].reshape(span, head_count, HD)
        own_seg = lax.dynamic_slice_in_dim(seg_query, offset, block_rows, 0)
        up_one = lax.dynamic_slice_in_dim(parent_one, offset, block_rows, 0)
        up_two = lax.dynamic_slice_in_dim(parent_two, offset, block_rows, 0)
        near_seg = lax.dynamic_slice_in_dim(seg_keys, offset, span, 0)
        gap = WINDOW + query_spots[:, None] - key_spots[None, :]
        same_path = (
            (near_seg[None, :] == own_seg[:, None])
            | (near_seg[None, :] == up_one[:, None])
            | (near_seg[None, :] == up_two[:, None])
        )
        allowed = (gap >= 0) & (gap < WINDOW) & same_path
        raw = (
            jnp.einsum("qhd,khd->hqk", query_block, key_block, preferred_element_type=jnp.float32)
            * scaling
        )
        return (jnp.where(allowed[None], raw, masked_score), query_block, key_block, value_block)

    def forward_block(block_index):
        scores, query_block, key_block, value_block = scores_of(block_index * block_rows)
        row_max = jnp.max(scores, axis=-1, keepdims=True)
        exponent = jnp.exp(scores - row_max)
        denominator = jnp.sum(exponent, axis=-1, keepdims=True)
        weights = (exponent / denominator).astype(jnp.bfloat16)
        mixed = jnp.einsum("hqk,khd->qhd", weights, value_block, preferred_element_type=jnp.float32)
        return (
            mixed.reshape(block_rows, head_width).astype(jnp.bfloat16),
            (row_max + jnp.log(denominator))[..., 0],
        )

    context_blocks, logsum_blocks = lax.map(forward_block, jnp.arange(block_count, dtype=jnp.int32))
    context = context_blocks.reshape(token_count, head_width)
    middle = inputs + lax.psum_scatter(
        jnp.dot(context, full_out, preferred_element_type=jnp.float32).astype(jnp.bfloat16),
        "tensor",
        scatter_dimension=0,
        tiled=True,
    ).astype(jnp.float32)
    factor_two = row_scale(middle)
    hat_two = middle * factor_two
    normed_two = (hat_two * gain_two).astype(jnp.bfloat16)
    normed_two_all = lax.all_gather(normed_two, "tensor", axis=0, tiled=True)
    upper = jnp.dot(normed_two_all, full_up, preferred_element_type=jnp.float32)
    active = gelu_exact(upper).astype(jnp.bfloat16)
    result = middle + lax.psum_scatter(
        jnp.dot(active, full_down, preferred_element_type=jnp.float32).astype(jnp.bfloat16),
        "tensor",
        scatter_dimension=0,
        tiled=True,
    ).astype(jnp.float32)
    incoming = cotangent.astype(jnp.float32)
    incoming_all = lax.all_gather(cotangent, "tensor", axis=0, tiled=True)
    grad_down = jnp.einsum("tf,td->fd", active, incoming_all, preferred_element_type=jnp.float32)
    grad_active = jnp.einsum(
        "td,fd->tf", incoming_all, full_down, preferred_element_type=jnp.float32
    )
    unused_value, gelu_pull = jax.vjp(gelu_exact, upper)
    grad_upper = gelu_pull(grad_active)[0].astype(jnp.bfloat16)
    grad_up = jnp.einsum(
        "tc,tf->cf", normed_two_all, grad_upper, preferred_element_type=jnp.float32
    )
    grad_normed_two = lax.psum_scatter(
        jnp.einsum("tf,cf->tc", grad_upper, full_up, preferred_element_type=jnp.float32).astype(
            jnp.bfloat16
        ),
        "tensor",
        scatter_dimension=0,
        tiled=True,
    ).astype(jnp.float32)
    through_two, gain_two_part = norm_backward(grad_normed_two, hat_two, factor_two, gain_two)
    grad_middle = incoming + through_two
    grad_middle_all = lax.all_gather(grad_middle.astype(jnp.bfloat16), "tensor", axis=0, tiled=True)
    grad_out = jnp.einsum("tc,td->cd", context, grad_middle_all, preferred_element_type=jnp.float32)
    grad_context = jnp.einsum(
        "td,cd->tc", grad_middle_all, full_out, preferred_element_type=jnp.float32
    ).astype(jnp.bfloat16)

    def backward_block(block_index, carry):
        grad_queries, grad_pairs = carry
        offset = block_index * block_rows
        scores, query_block, key_block, value_block = scores_of(offset)
        logsum = lax.dynamic_index_in_dim(logsum_blocks, block_index, 0, keepdims=False)
        probs = jnp.exp(scores - logsum[..., None])
        grad_rows = lax.dynamic_slice_in_dim(grad_context, offset, block_rows, 0).reshape(
            block_rows, head_count, HD
        )
        grad_probs = jnp.einsum(
            "qhd,khd->hqk", grad_rows, value_block, preferred_element_type=jnp.float32
        )
        inner = jnp.sum(probs * grad_probs, axis=-1, keepdims=True)
        grad_scores = (probs * (grad_probs - inner)).astype(jnp.bfloat16)
        grad_query_block = (
            jnp.einsum("hqk,khd->qhd", grad_scores, key_block, preferred_element_type=jnp.float32)
            * scaling
        )
        grad_key_block = (
            jnp.einsum("hqk,qhd->khd", grad_scores, query_block, preferred_element_type=jnp.float32)
            * scaling
        )
        grad_value_block = jnp.einsum(
            "hqk,qhd->khd",
            probs.astype(jnp.bfloat16),
            grad_rows,
            preferred_element_type=jnp.float32,
        )
        grad_queries = lax.dynamic_update_slice_in_dim(
            grad_queries, grad_query_block.reshape(block_rows, head_width), offset, 0
        )
        update = jnp.concatenate(
            [grad_key_block.reshape(span, head_width), grad_value_block.reshape(span, head_width)],
            axis=1,
        )
        current = lax.dynamic_slice_in_dim(grad_pairs, offset, span, 0)
        grad_pairs = lax.dynamic_update_slice_in_dim(grad_pairs, current + update, offset, 0)
        return (grad_queries, grad_pairs)

    start_carry = (
        jnp.zeros((token_count, head_width), jnp.float32),
        jnp.zeros((WINDOW + token_count, 2 * head_width), jnp.float32),
    )
    grad_queries, grad_pairs = lax.fori_loop(0, block_count, backward_block, start_carry)
    grad_own = grad_pairs[WINDOW:]
    for distance in range(1, hop_count + 1):
        length = min(token_count, WINDOW - (distance - 1) * token_count)
        first_row = WINDOW - (distance - 1) * token_count - length
        piece = grad_pairs[first_row : first_row + length]
        returned = from_behind(piece.astype(jnp.bfloat16), "dp", -distance).astype(piece.dtype)
        grad_own = grad_own + jnp.pad(returned, ((token_count - length, 0), (0, 0)))
    grad_keys = grad_own[:, :head_width].astype(jnp.bfloat16)
    grad_values = grad_own[:, head_width:].astype(jnp.bfloat16)
    grad_queries_low = grad_queries.astype(jnp.bfloat16)
    grad_query = jnp.einsum(
        "tc,tq->cq", normed_all, grad_queries_low, preferred_element_type=jnp.float32
    )
    grad_key = jnp.einsum("tc,tq->cq", normed_all, grad_keys, preferred_element_type=jnp.float32)
    grad_value = jnp.einsum(
        "tc,tq->cq", normed_all, grad_values, preferred_element_type=jnp.float32
    )
    part_query = jnp.einsum(
        "tq,cq->tc", grad_queries_low, full_query, preferred_element_type=jnp.float32
    )
    part_key = jnp.einsum("tq,cq->tc", grad_keys, full_key, preferred_element_type=jnp.float32)
    part_value = jnp.einsum(
        "tq,cq->tc", grad_values, full_value, preferred_element_type=jnp.float32
    )
    grad_normed = lax.psum_scatter(
        (part_query + part_key + part_value).astype(jnp.bfloat16),
        "tensor",
        scatter_dimension=0,
        tiled=True,
    ).astype(jnp.float32)
    through_one, gain_one_part = norm_backward(grad_normed, hat_one, factor_one, gain_one)
    grad_inputs = grad_middle + through_one
    gain_one_sum, gain_two_sum = lax.psum((gain_one_part, gain_two_part), "tensor")
    summed = (
        *side_by_side(
            (
                gain_one_sum.astype(jnp.bfloat16),
                grad_query.astype(jnp.bfloat16),
                grad_key.astype(jnp.bfloat16),
                grad_value.astype(jnp.bfloat16),
            ),
            "dp",
            0,
            1,
        ),
        sum_at_owner(grad_out.astype(jnp.bfloat16), "dp", 1),
        *side_by_side(
            (gain_two_sum.astype(jnp.bfloat16), grad_up.astype(jnp.bfloat16)), "dp", 0, 1
        ),
        sum_at_owner(grad_down.astype(jnp.bfloat16), "dp", 1),
    )
    return (
        result.astype(jnp.bfloat16),
        grad_inputs.astype(jnp.bfloat16),
        summed[0],
        summed[1],
        summed[2],
        summed[3],
        summed[4],
        summed[5],
        summed[6],
        summed[7],
    )


def solution(mesh):
    return jax.shard_map(
        shards,
        mesh=mesh,
        in_specs=(
            P(("dp", "tensor"), None),
            P(("dp", "tensor"), None),
            P(),
            P(),
            P("dp"),
            P("dp", "tensor"),
            P("dp", "tensor"),
            P("dp", "tensor"),
            P("tensor", "dp"),
            P("dp"),
            P("dp", "tensor"),
            P("tensor", "dp"),
        ),
        out_specs=(
            P(("dp", "tensor"), None),
            P(("dp", "tensor"), None),
            P("dp"),
            P("dp", "tensor"),
            P("dp", "tensor"),
            P("dp", "tensor"),
            P("tensor", "dp"),
            P("dp"),
            P("dp", "tensor"),
            P("tensor", "dp"),
        ),
        check_vma=False,
    )
```

profile of v0, /device:TPU:0, one launch (start us, length us, event | category | flops | bytes accessed | tf_op | source)
XLA Modules:
  0.0 772.6 jit_solution(16327131825716059331)
XLA Ops:
  12.9 23.7 %all-reduce.5 = (bf16[768]{0:T(1024)(128)(2,1)S(1)}, bf16[768]{0:T(1024)(128)(2,1)}) all-reduce(bf16[768]{0:T(1024)(128)(2,1)S(1)} %dynamic-update-slice, bf16[768]{0:T(1024)(128)(2,1)S(1)} %dynamic-update-slice.1), channel_id=1, replica_groups=mesh['dp'=8,'tensor'=4] {'dp'}, use_global_device_ids=true, to_apply=%add.2 | all-reduce | flops 1536 | bytes 6144
  41.0 31.2 %all_gather.38 = bf16[768,192]{1,0:T(8,128)(2,1)S(1)} all-gather(bf16[96,192]{1,0:T(8,128)(2,1)} %param.22), channel_id=1, replica_groups=mesh['dp'=8,'tensor'=4] {'dp'}, dimensions={0}, use_global_device_ids=true | all-gather | bytes 331776 | tf_op jit(solution)/shard_map/all_gather | solution.py:78
  72.2 31.2 %all_gather.39 = bf16[768,192]{1,0:T(8,128)(2,1)S(1)} all-gather(bf16[96,192]{1,0:T(8,128)(2,1)} %param.23), channel_id=1, replica_groups=mesh['dp'=8,'tensor'=4] {'dp'}, dimensions={0}, use_global_device_ids=true | all-gather | bytes 331776 | tf_op jit(solution)/shard_map/all_gather | solution.py:79
  110.2 46.0 %all_gather.41 = bf16[192,768]{0,1:T(8,128)(2,1)} all-gather(bf16[192,96]{0,1:T(8,128)(2,1)S(1)} %copy.48), channel_id=1, replica_groups=mesh['dp'=8,'tensor'=4] {'dp'}, dimensions={1}, use_global_device_ids=true | all-gather | bytes 331776 | tf_op jit(solution)/shard_map/all_gather | solution.py:80
  156.2 31.0 %all_gather.40 = bf16[768,192]{1,0:T(8,128)(2,1)S(1)} all-gather(bf16[96,192]{1,0:T(8,128)(2,1)S(1)} %copy-done.35), channel_id=1, replica_groups=mesh['dp'=8,'tensor'=4] {'dp'}, dimensions={0}, use_global_device_ids=true | all-gather | bytes 331776 | tf_op jit(solution)/shard_map/all_gather | solution.py:77
  193.2 72.5 %while.29 = (s32[]{:T(128)}, bf16[2,640,192]{1,2,0:T(8,128)(2,1)}, f32[2,3,640]{2,1,0:T(4,128)S(1)}, s32[2]{0:T(128)S(1)}, bf16[2816,384]{0,1:T(8,128)(2,1)}, /*...) while((s32[]{:T(128)}, bf16[2,640,192]{1,2,0:T(8,128)(2,1)}, ...), condition=%wide.region_6.7_spmd.clone, body=%wide.region_3.6_spmd.clone.sunk | while | flops 1133730560 | bytes 66249560 | solution.py:163
  201.3 8.0 %fusion.136 = (f32[3,640]{1,0:T(4,128)S(1)}, f32[3,640,2176]{2,1,0:T(8,128)}) fusion(pred[640,2176]{1,0:T(8,128)(4,1)S(1)} %fusion.135, bf16[640,3,64]{0,2,1:T(8,128)(2,1)S(1)} %bitcast.146, bf16[2176,3,64]{0,2,1:T(8,128)(2,1)S(1)} %bitcast.145), kind=kOutput, calls=%fused_computation.7.clone.1 | convolution fusion | flops 547305600 | bytes 19193344 | tf_op jit(solution)/shard_map/while/body/eval_jaxpr/qhd,khd->hqk/dot_general | solution.py:146
  209.3 10.5 %fusion.137 = f32[3,640]{1,0:T(4,128)S(1)} fusion(f32[3,640,2176]{2,1,0:T(8,128)} %get-tuple-element.566, f32[3,640]{1,0:T(4,128)S(1)} %get-tuple-element.567, pred[640,2176]{1,0:T(8,128)(4,1)S(1)} %fusion.135), kind=kLoop, calls=%fused_computation.8.clone.1 | loop fusion | flops 16709760 | bytes 18119680 | tf_op jit(solution)/shard_map/while/body/eval_jaxpr/reduce_sum | solution.py:155
  219.8 8.8 %fusion.138 = bf16[3,64,640]{2,1,0:T(8,128)(2,1)S(1)} fusion(bf16[2176,3,64]{0,2,1:T(8,128)(2,1)S(1)} %bitcast.144, f32[3,640,2176]{2,1,0:T(8,128)} %get-tuple-element.566, f32[3,640]{1,0:T(4,128)S(1)} %fusion.137, f32[3,640]{1,0:T(4,128)S(1)} %get-tuple-element.567, pred[640,2176]{1,0:T(8,128)(4,1)S(1)} %fusion.135), kind=kOutput, calls=%fused_computation.15.clone.1 | convolution fusion | flops 555786240 | bytes 19201024 | tf_op jit(solution)/shard_map/while/body/eval_jaxpr/hqk,khd->qhd/dot_general | solution.py:157
  237.5 8.0 %fusion.136 = (f32[3,640]{1,0:T(4,128)S(1)}, f32[3,640,2176]{2,1,0:T(8,128)}) fusion(pred[640,2176]{1,0:T(8,128)(4,1)S(1)} %fusion.135, bf16[640,3,64]{0,2,1:T(8,128)(2,1)S(1)} %bitcast.146, bf16[2176,3,64]{0,2,1:T(8,128)(2,1)S(1)} %bitcast.145), kind=kOutput, calls=%fused_computation.7.clone.1 | convolution fusion | flops 547305600 | bytes 19193344 | tf_op jit(solution)/shard_map/while/body/eval_jaxpr/qhd,khd->hqk/dot_general | solution.py:146
  245.5 10.5 %fusion.137 = f32[3,640]{1,0:T(4,128)S(1)} fusion(f32[3,640,2176]{2,1,0:T(8,128)} %get-tuple-element.566, f32[3,640]{1,0:T(4,128)S(1)} %get-tuple-element.567, pred[640,2176]{1,0:T(8,128)(4,1)S(1)} %fusion.135), kind=kLoop, calls=%fused_computation.8.clone.1 | loop fusion | flops 16709760 | bytes 18119680 | tf_op jit(solution)/shard_map/while/body/eval_jaxpr/reduce_sum | solution.py:155
  256.0 8.9 %fusion.138 = bf16[3,64,640]{2,1,0:T(8,128)(2,1)S(1)} fusion(bf16[2176,3,64]{0,2,1:T(8,128)(2,1)S(1)} %bitcast.144, f32[3,640,2176]{2,1,0:T(8,128)} %get-tuple-element.566, f32[3,640]{1,0:T(4,128)S(1)} %fusion.137, f32[3,640]{1,0:T(4,128)S(1)} %get-tuple-element.567, pred[640,2176]{1,0:T(8,128)(4,1)S(1)} %fusion.135), kind=kOutput, calls=%fused_computation.15.clone.1 | convolution fusion | flops 555786240 | bytes 19201024 | tf_op jit(solution)/shard_map/while/body/eval_jaxpr/hqk,khd->qhd/dot_general | solution.py:157
  271.0 32.7 %reduce-scatter.5.cloned.1.call-done = bf16[320,768]{1,0:T(8,128)(2,1)} async-done(((bf16[1280,768]{1,0:T(8,128)(2,1)}), bf16[320,768]{1,0:T(8,128)(2,1)}) %reduce-scatter.5.cloned.1.call-update) | async-done | bytes 491536 | tf_op jit(solution)/shard_map/reduce_scatter | solution.py:165
  308.4 8.9 %all-gather.11.cloned.1.call-done = bf16[768,768]{1,0:T(8,128)(2,1)} async-done(((bf16[96,768]{1,0:T(8,128)(2,1)}), bf16[768,768]{1,0:T(8,128)(2,1)}) %all-gather.11.cloned.1.call-update) | async-done | bytes 1179664 | tf_op jit(solution)/shard_map/all_gather | solution.py:82
  317.4 22.3 %all-gather.9.cloned.1.call-done = bf16[1280,768]{1,0:T(8,128)(2,1)} async-done(((bf16[320,768]{1,0:T(8,128)(2,1)}), bf16[1280,768]{1,0:T(8,128)(2,1)}) %all-gather.9.cloned.1.call-update) | async-done | bytes 1966096 | tf_op jit(solution)/shard_map/all_gather | solution.py:174
  345.1 38.4 %all-gather.13.cloned.1.call-done = bf16[768,768]{0,1:T(8,128)(2,1)} async-done(((bf16[768,96]{0,1:T(8,128)(2,1)}), bf16[768,768]{0,1:T(8,128)(2,1)}) %all-gather.13.cloned.1.call-update) | async-done | bytes 1179664 | tf_op jit(solution)/shard_map/all_gather | solution.py:83
  383.5 21.9 %all-gather.15.cloned.1.call-done = bf16[1280,768]{1,0:T(8,128)(2,1)} async-done(((bf16[320,768]{1,0:T(8,128)(2,1)}), bf16[1280,768]{1,0:T(8,128)(2,1)}) %all-gather.15.cloned.1.call-update) | async-done | bytes 1966096 | tf_op jit(solution)/shard_map/all_gather | solution.py:184
  405.4 13.1 %add_convert_fusion = (bf16[1280,768]{1,0:T(8,128)(2,1)S(1)}, f32[1280,768]{1,0:T(8,128)}) fusion(f32[1280,768]{1,0:T(8,128)} %fusion.64, bf16[1280,768]{1,0:T(8,128)(2,1)} %all-gather.15.cloned.1.call-done, bf16[768,768]{0,1:T(8,128)(2,1)} %all-gather.13.cloned.1.call-done), kind=kOutput, calls=%fused_computation.47 | convolution fusion | flops 1580728320 | bytes 12976128 | tf_op jit(solution)/shard_map/td,fd->tf/dot_general | solution.py:186
  424.3 30.7 %reduce-scatter.9.cloned.1.call-done = bf16[320,768]{1,0:T(8,128)(2,1)} async-done(((bf16[1280,768]{1,0:T(8,128)(2,1)}), bf16[320,768]{1,0:T(8,128)(2,1)}) %reduce-scatter.9.cloned.1.call-update) | async-done | bytes 491536 | tf_op jit(solution)/shard_map/reduce_scatter | solution.py:194
  459.9 21.4 %all-gather.17.cloned.1.call-done = bf16[1280,768]{1,0:T(8,128)(2,1)} async-done(((bf16[320,768]{1,0:T(8,128)(2,1)}), bf16[1280,768]{1,0:T(8,128)(2,1)}) %all-gather.17.cloned.1.call-update) | async-done | bytes 1966096 | tf_op jit(solution)/shard_map/all_gather | solution.py:204
  487.6 112.6 %while.30 = (s32[]{:T(128)}, bf16[1280,192]{0,1:T(8,128)(2,1)}, f32[2816,384]{0,1:T(8,128)}, bf16[2816,384]{0,1:T(8,128)(2,1)}, s32[2816]{0:T(1024)S(1)}, /*inde...) while((s32[]{:T(128)}, bf16[1280,192]{0,1:T(8,128)(2,1)}, ...), condition=%wide.region_14.15_spmd.clone, body=%wide.region_12.14_spmd.clone.sunk | while | flops 2727729920 | bytes 220916592 | solution.py:253
  495.2 8.1 %fusion.150 = f32[3,640,2176]{2,1,0:T(8,128)} fusion(bf16[640,3,64]{0,2,1:T(8,128)(2,1)S(1)} %bitcast.141, bf16[2176,3,64]{0,2,1:T(8,128)(2,1)S(1)} %bitcast.140), kind=kOutput, calls=%fused_computation.138.clone.1 | convolution fusion | flops 534773760 | bytes 17793024 | tf_op jit(solution)/shard_map/while/body/eval_jaxpr/qhd,khd->hqk/dot_general | solution.py:219
  503.3 15.1 %multiply_reduce_fusion.3 = (f32[3,640]{1,0:T(4,128)S(1)}, f32[3,640,2176]{2,1,0:T(8,128)}) fusion(f32[3,640,2176]{2,1,0:T(8,128)} %fusion.150, f32[3,640]{1,0:T(4,128)S(1)} %dynamic-slice_bitcast_fusion.2, bf16[640,3,64]{0,2,1:T(8,128)(2,1)S(1)} %bitcast.138, bf16[2176,3,64]{0,2,1:T(8,128)(2,1)S(1)} %bitcast.135, pred[640,2176]{1,0:T(8,128)(4,1)S(1)} %fusion.151), kind=kOutput, calls=%fused_computation.24.clone.1 | convolution fusion | flops 555661440 | bytes 35912704 | tf_op jit(solution)/shard_map/while/body/eval_jaxpr/qhd,khd->hqk/dot_general | solution.py:146
  518.5 11.4 %multiply_convert_fusion.4 = bf16[3,640,2176]{2,1,0:T(8,128)(2,1)S(1)} fusion(f32[3,640,2176]{2,1,0:T(8,128)} %get-tuple-element.583, f32[3,640,2176]{2,1,0:T(8,128)} %fusion.150, f32[3,640]{1,0:T(4,128)S(1)} %get-tuple-element.584), kind=kLoop, calls=%fused_computation.23.clone.1 | loop fusion | flops 12533760 | bytes 41786880 | tf_op jit(solution)/shard_map/while/body/eval_jaxpr/convert_element_type | solution.py:223
  551.5 8.1 %fusion.150 = f32[3,640,2176]{2,1,0:T(8,128)} fusion(bf16[640,3,64]{0,2,1:T(8,128)(2,1)S(1)} %bitcast.141, bf16[2176,3,64]{0,2,1:T(8,128)(2,1)S(1)} %bitcast.140), kind=kOutput, calls=%fused_computation.138.clone.1 | convolution fusion | flops 534773760 | bytes 17793024 | tf_op jit(solution)/shard_map/while/body/eval_jaxpr/qhd,khd->hqk/dot_general | solution.py:219
  559.6 15.1 %multiply_reduce_fusion.3 = (f32[3,640]{1,0:T(4,128)S(1)}, f32[3,640,2176]{2,1,0:T(8,128)}) fusion(f32[3,640,2176]{2,1,0:T(8,128)} %fusion.150, f32[3,640]{1,0:T(4,128)S(1)} %dynamic-slice_bitcast_fusion.2, bf16[640,3,64]{0,2,1:T(8,128)(2,1)S(1)} %bitcast.138, bf16[2176,3,64]{0,2,1:T(8,128)(2,1)S(1)} %bitcast.135, pred[640,2176]{1,0:T(8,128)(4,1)S(1)} %fusion.151), kind=kOutput, calls=%fused_computation.24.clone.1 | convolution fusion | flops 555661440 | bytes 35912704 | tf_op jit(solution)/shard_map/while/body/eval_jaxpr/qhd,khd->hqk/dot_general | solution.py:146
  574.7 11.4 %multiply_convert_fusion.4 = bf16[3,640,2176]{2,1,0:T(8,128)(2,1)S(1)} fusion(f32[3,640,2176]{2,1,0:T(8,128)} %get-tuple-element.583, f32[3,640,2176]{2,1,0:T(8,128)} %fusion.150, f32[3,640]{1,0:T(4,128)S(1)} %get-tuple-element.584), kind=kLoop, calls=%fused_computation.23.clone.1 | loop fusion | flops 12533760 | bytes 41786880 | tf_op jit(solution)/shard_map/while/body/eval_jaxpr/convert_element_type | solution.py:223
  606.3 27.3 %collective-permute-done.3 = bf16[256,384]{0,1:T(8,128)(2,1)S(1)} collective-permute-done((bf16[256,384]{0,1:T(8,128)(2,1)S(1)}, bf16[256,384]{0,1:T(8,128)(2,1)S(1)}, u32[]{:S(2)}, u32[]{:S(2)}) %collective-permute-start.3) | collective-permute-done | bytes 196640 | tf_op jit(solution)/shard_map/ppermute | solution.py:16
  667.0 11.4 %all-to-all-done.3 = bf16[8,768,96]{1,2,0:T(8,128)(2,1)} async-done(((bf16[8,768,96]{1,2,0:T(8,128)(2,1)}), bf16[8,768,96]{1,2,0:T(8,128)(2,1)}, u32[]{:S(2)}, u32[]{:S(2)}) %all-to-all-start.3) | async-done | bytes 1179680 | tf_op jit(solution)/shard_map/all_to_all | solution.py:27
  686.5 6.5 all-reduce.4
  710.6 15.5 %all-to-all-done = bf16[8,96,577]{2,1,0:T(8,128)(2,1)S(1)} async-done(((bf16[8,96,577]{2,1,0:T(8,128)(2,1)}), bf16[8,96,577]{2,1,0:T(8,128)(2,1)S(1)}, u32[]{:S(2)}, u32[]{:S(2)}) %all-to-all-start) | async-done | bytes 886304 | tf_op jit(solution)/shard_map/all_to_all | solution.py:27
  739.1 24.3 %all-to-all-done.2 = bf16[8,96,769]{2,1,0:T(8,128)(2,1)S(1)} async-done(((bf16[8,96,769]{2,1,0:T(8,128)(2,1)}), bf16[8,96,769]{2,1,0:T(8,128)(2,1)S(1)}, u32[]{:S(2)}, u32[]{:S(2)}) %all-to-all-start.2) | async-done | bytes 1181216 | tf_op jit(solution)/shard_map/all_to_all | solution.py:27
  (258 shorter events, 192.4 us)
Async XLA Ops:
  8.0 95.4 %all-gather.7.cloned.1.call-start = ((), (), s32[]{:S(2)}) async-start(), calls=%async_computation.8 | async-start | bytes 2457600 | tf_op jit(solution)/shard_map/all_gather | solution.py:101
  9.3 30.9 %copy-start.36 = (f32[320]{0:T(512)}, f32[320]{0:T(512)S(1)}, u32[]{:S(2)}) copy-start(f32[320]{0:T(512)S(1)} %add_rsqrt_fusion.1) | copy-start | bytes 3844
  39.2 264.5 %reduce-scatter.5.cloned.1.call-start = ((), (), s32[]{:S(2)}) async-start(), calls=%async_computation.9 | async-start | bytes 2457600 | tf_op jit(solution)/shard_map/reduce_scatter | solution.py:165
  72.2 36.3 %copy-start.19 = (bf16[768,192]{1,0:T(8,128)(2,1)}, bf16[768,192]{1,0:T(8,128)(2,1)S(1)}, u32[]{:S(2)}) copy-start(bf16[768,192]{1,0:T(8,128)(2,1)S(1)} %all_gather.38) | copy-start | bytes 884740
  103.4 52.9 %copy-start.21 = (bf16[768,192]{1,0:T(8,128)(2,1)}, bf16[768,192]{1,0:T(8,128)(2,1)S(1)}, u32[]{:S(2)}) copy-start(bf16[768,192]{1,0:T(8,128)(2,1)S(1)} %all_gather.39) | copy-start | bytes 884740
  103.4 52.9 %copy-start.35 = (bf16[96,192]{1,0:T(8,128)(2,1)S(1)}, bf16[96,192]{1,0:T(8,128)(2,1)}, u32[]{:S(2)}) copy-start(bf16[96,192]{1,0:T(8,128)(2,1)} %param.21) | copy-start | bytes 110596
  105.9 82.6 %copy-start.3 = (bf16[1280,768]{1,0:T(8,128)(2,1)S(1)}, bf16[1280,768]{1,0:T(8,128)(2,1)}, u32[]{:S(2)}) copy-start(bf16[1280,768]{1,0:T(8,128)(2,1)} %all-gather.7.cloned.1.call-done) | copy-start | bytes 5898244
  108.5 83.2 %collective-permute-start.1 = (bf16[1280,384]{0,1:T(8,128)(2,1)S(1)}, bf16[1280,384]{0,1:T(8,128)(2,1)S(1)}, u32[]{:S(2)}, u32[]{:S(2)}) collective-permute-start(bf16[1280,384]{0,1:T(8,128)(2,1)S(1)} %pad_maximum_fusion.1), channel_id=1, source_target_pairs={{0,4},{4,8},{8,12},{12,16},{16,20},{20,24},{24,28},{1,5},{5,9},{9,... | collective-permute-start | bytes 2949128 | tf_op jit(solution)/shard_map/ppermute | solution.py:16
  187.2 4.5 collective-permute-start
  265.7 38.0 %copy-start.1 = (bf16[320,768]{1,0:T(8,128)(2,1)S(1)}, bf16[320,768]{1,0:T(8,128)(2,1)}, u32[]{:S(2)}) copy-start(bf16[320,768]{1,0:T(8,128)(2,1)} %param.16) | copy-start | bytes 1474564
  266.9 40.2 %copy-start.10 = (bf16[2,24,8,640]{3,2,0,1:T(8,128)(2,1)}, bf16[2,24,8,640]{3,2,0,1:T(8,128)(2,1)S(1)}, u32[]{:S(2)}) copy-start(bf16[2,24,8,640]{3,2,0,1:T(8,128)(2,1)S(1)} %copy.67) | copy-start | bytes 1474564
  270.1 47.3 %all-gather.11.cloned.1.call-start = ((), (), s32[]{:S(2)}) async-start(), calls=%async_computation.11 | async-start | bytes 1327104 | tf_op jit(solution)/shard_map/all_gather | solution.py:82
  270.7 69.0 %all-gather.9.cloned.1.call-start = ((), (), s32[]{:S(2)}) async-start(), calls=%async_computation.10 | async-start | bytes 2457600 | tf_op jit(solution)/shard_map/all_gather | solution.py:174
  271.0 186.2 %copy-start.29 = (f32[768]{0:T(1024)}, f32[768]{0:T(1024)S(1)}, u32[]{:S(2)}) copy-start(f32[768]{0:T(1024)S(1)} %convert_element_type.159) | copy-start | bytes 9220
  305.0 152.2 %copy-start.33 = (f32[320]{0:T(512)}, f32[320]{0:T(512)S(1)}, u32[]{:S(2)}) copy-start(f32[320]{0:T(512)S(1)} %add_rsqrt_fusion) | copy-start | bytes 3844
  307.1 76.4 %all-gather.13.cloned.1.call-start = ((), (), s32[]{:S(2)}) async-start(), calls=%async_computation.12 | async-start | bytes 1327104 | tf_op jit(solution)/shard_map/all_gather | solution.py:83
  307.6 97.7 %all-gather.15.cloned.1.call-start = ((), (), s32[]{:S(2)}) async-start(), calls=%async_computation.14 | async-start | bytes 2457600 | tf_op jit(solution)/shard_map/all_gather | solution.py:184
  308.4 146.7 %reduce-scatter.9.cloned.1.call-start = ((), (), s32[]{:S(2)}) async-start(), calls=%async_computation.15 | async-start | bytes 2457600 | tf_op jit(solution)/shard_map/reduce_scatter | solution.py:194
  419.8 35.2 %copy-start.5 = (bf16[320,768]{1,0:T(8,128)(2,1)S(1)}, bf16[320,768]{1,0:T(8,128)(2,1)}, u32[]{:S(2)}) copy-start(bf16[320,768]{1,0:T(8,128)(2,1)} %reduce-scatter.5.cloned.1.call-done) | copy-start | bytes 1474564
  419.8 37.4 %copy-start.7 = (bf16[320,768]{1,0:T(8,128)(2,1)S(1)}, bf16[320,768]{1,0:T(8,128)(2,1)}, u32[]{:S(2)}) copy-start(bf16[320,768]{1,0:T(8,128)(2,1)} %param.17) | copy-start | bytes 1474564
  424.2 57.0 %copy-start.25 = (bf16[192,768]{0,1:T(8,128)(2,1)S(1)}, bf16[192,768]{0,1:T(8,128)(2,1)}, u32[]{:S(2)}) copy-start(bf16[192,768]{0,1:T(8,128)(2,1)} %all_gather.41) | copy-start | bytes 884740
  424.2 57.0 %all-gather.17.cloned.1.call-start = ((), (), s32[]{:S(2)}) async-start(), calls=%async_computation.16 | async-start | bytes 2457600 | tf_op jit(solution)/shard_map/all_gather | solution.py:204
  457.2 30.4 %copy-start.38 = (f32[320]{0:T(512)}, f32[320]{0:T(512)S(1)}, u32[]{:S(2)}) copy-start(f32[320]{0:T(512)S(1)} %broadcast_multiply_fusion.1) | copy-start | bytes 3844
  459.4 225.5 %reduce-scatter.11.cloned.1.call-start = ((), (), s32[]{:S(2)}) async-start(), calls=%async_computation.17 | async-start | bytes 2457600 | tf_op jit(solution)/shard_map/reduce_scatter | solution.py:278
  602.8 30.9 %collective-permute-start.2 = (bf16[1280,384]{0,1:T(8,128)(2,1)S(1)}, bf16[1280,384]{0,1:T(8,128)(2,1)S(1)}, u32[]{:S(2)}, u32[]{:S(2)}) collective-permute-start(bf16[1280,384]{0,1:T(8,128)(2,1)S(1)} %slice.58), channel_id=1, source_target_pairs={{4,0},{8,4},{12,8},{16,12},{20,16},{24,20},{28,24},{5,1},{9,5},{13... | collective-permute-start | bytes 2949128 | tf_op jit(solution)/shard_map/ppermute | solution.py:16
  604.3 29.4 %collective-permute-start.3 = (bf16[256,384]{0,1:T(8,128)(2,1)S(1)}, bf16[256,384]{0,1:T(8,128)(2,1)S(1)}, u32[]{:S(2)}, u32[]{:S(2)}) collective-permute-start(bf16[256,384]{0,1:T(8,128)(2,1)S(1)} %slice.59), channel_id=1, source_target_pairs={{8,0},{12,4},{16,8},{20,12},{24,16},{28,20},{9,1},{13,5},{17,9},{2... | collective-permute-start | bytes 589832 | tf_op jit(solution)/shard_map/ppermute | solution.py:16
  605.6 29.9 %copy-start.20 = (bf16[768,192]{1,0:T(8,128)(2,1)S(1)}, bf16[768,192]{1,0:T(8,128)(2,1)}, u32[]{:S(2)}) copy-start(bf16[768,192]{1,0:T(8,128)(2,1)} %copy-done.19) | copy-start | bytes 884740
  645.7 32.7 %all-to-all-start.3 = ((bf16[8,768,96]{1,2,0:T(8,128)(2,1)}), bf16[8,768,96]{1,2,0:T(8,128)(2,1)}, u32[]{:S(2)}, u32[]{:S(2)}) async-start(bf16[8,768,96]{1,2,0:T(8,128)(2,1)} %bitcast.154), calls=%async_computation.7 | async-start | bytes 2359296 | tf_op jit(solution)/shard_map/all_to_all | solution.py:27
  650.0 84.5 %reduce-scatter.7.cloned.1.call-start = ((), (), s32[]{:S(2)}) async-start(), calls=%async_computation.13 | async-start | bytes 2457600 | tf_op jit(solution)/shard_map/reduce_scatter | solution.py:177
  678.4 17.6 %all-to-all-start.1 = ((bf16[8,192,96]{2,1,0:T(8,128)(2,1)}), bf16[8,192,96]{2,1,0:T(8,128)(2,1)}, u32[]{:S(2)}, u32[]{:S(2)}) async-start(bf16[8,192,96]{2,1,0:T(8,128)(2,1)} %bitcast.150), calls=%async_computation.5 | async-start | bytes 786432 | tf_op jit(solution)/shard_map/all_to_all | solution.py:27
  696.0 30.0 %all-to-all-start = ((bf16[8,96,577]{2,1,0:T(8,128)(2,1)}), bf16[8,96,577]{2,1,0:T(8,128)(2,1)S(1)}, u32[]{:S(2)}, u32[]{:S(2)}) async-start(bf16[8,96,577]{2,1,0:T(8,128)(2,1)} %pad_maximum_fusion.2), calls=%async_computation.4 | async-start | bytes 1966080 | tf_op jit(solution)/shard_map/all_to_all | solution.py:27
  727.0 36.4 %all-to-all-start.2 = ((bf16[8,96,769]{2,1,0:T(8,128)(2,1)}), bf16[8,96,769]{2,1,0:T(8,128)(2,1)S(1)}, u32[]{:S(2)}, u32[]{:S(2)}) async-start(bf16[8,96,769]{2,1,0:T(8,128)(2,1)} %pad_maximum_fusion), calls=%async_computation.6 | async-start | bytes 2752512 | tf_op jit(solution)/shard_map/all_to_all | solution.py:27
  (36 other events, 395.1 us)
Sparse Core Ops, SparseCore 0:
  39.3 19.0 all-gather.6
  270.2 33.4 reduce-scatter.4
  424.4 30.6 reduce-scatter.8
  639.0 28.7 reduce-scatter.10
  670.4 30.8 reduce-scatter.6
Sparse Core Ops, SparseCore 1:
  273.0 44.3 all-gather.10
  319.5 20.1 all-gather.8
  342.0 41.5 all-gather.12
  385.2 20.1 all-gather.14
  459.5 21.7 all-gather.16
where the time goes:
time: 778 us; the launch traced here: 773 us
  waiting for transfers between devices  259 us (33%)
  blocking collectives  170 us (22%)
  matrix products  150 us (19%)
  other arithmetic  107 us (14%)
  local copies, waits for them, and re-layouts  43.4 us (6%)
  starting transfers between devices  24.5 us (3%)
  between operations  17 us (2%)
    all_to_all x4, waiting for transfers between devices, sum_at_owner(): lax.all_to_all(tiles, axis, split_axis=0, concat_axis=0, tiled=True)  51.2 us
    dot_general x4, matrix products, scores_of(): jnp.einsum('qhd,khd->hqk', query_block, key_block, preferred_element_type...  46.3 us
    all_gather x1, blocking collectives, shards(): lax.all_gather(w_out, 'dp', axis=1, tiled=True)  46 us
    all_gather x1, waiting for transfers between devices, shards(): lax.all_gather(w_down, 'dp', axis=1, tiled=True)  38.4 us
    reduce_scatter x1, waiting for transfers between devices, shards(): lax.psum_scatter(jnp.dot(context, full_out, preferred_element_type=jnp.fl...  32.7 us
    all_gather x1, blocking collectives, shards(): lax.all_gather(w_key, 'dp', axis=0, tiled=True)  31.2 us
    all_gather x1, blocking collectives, shards(): lax.all_gather(w_value, 'dp', axis=0, tiled=True)  31.2 us
    all_gather x1, blocking collectives, shards(): lax.all_gather(w_query, 'dp', axis=0, tiled=True)  31 us
  transfers between devices with their start and end apart: 18, of which 12 were waited for; matrix products, arithmetic and copies ran while one was open for 8% of the time, Pallas kernels for 0%

commit v1 on v0

--- a/solution.py
+++ b/solution.py
@@ -201,7 +201,11 @@
     ).astype(jnp.float32)
     through_two, gain_two_part = norm_backward(grad_normed_two, hat_two, factor_two, gain_two)
     grad_middle = incoming + through_two
-    grad_middle_all = lax.all_gather(grad_middle.astype(jnp.bfloat16), "tensor", axis=0, tiled=True)
+    value = grad_middle.astype(jnp.bfloat16)
+    n_dev = lax.axis_size("tensor")
+    blocks = jnp.stack([value for _ in range(n_dev)])
+    blocks = lax.all_to_all(blocks, "tensor", split_axis=0, concat_axis=0)
+    grad_middle_all = jnp.concatenate(blocks, axis=0)
     grad_out = jnp.einsum("tc,td->cd", context, grad_middle_all, preferred_element_type=jnp.float32)
     grad_context = jnp.einsum(
         "td,cd->tc", grad_middle_all, full_out, preferred_element_type=jnp.float32

time: 778 us -> 782 us (level)
    all_to_all x0 -> x1, waiting for transfers between devices: none -> 23.8 us  [shards(): blocks = lax.all_to_all(blocks, 'tensor', split_axis=0, concat_axis=0)]
    all_gather x1 -> x0, waiting for transfers between devices: 21.4 us -> none  [shards(): lax.all_gather(grad_middle.astype(jnp.bfloat16), 'tensor', axis=0, tiled=...]
where the time goes in v1:
time: 782 us; the launch traced here: 776 us
  waiting for transfers between devices  260 us (33%)
  blocking collectives  169 us (22%)
  matrix products  148 us (19%)
  other arithmetic  107 us (14%)
  local copies, waits for them, and re-layouts  44.8 us (6%)
  starting transfers between devices  28.1 us (4%)
  between operations  16.7 us (2%)
    all_to_all x4, waiting for transfers between devices, sum_at_owner(): lax.all_to_all(tiles, axis, split_axis=0, concat_axis=0, tiled=True)  50.8 us
    dot_general x4, matrix products, scores_of(): jnp.einsum('qhd,khd->hqk', query_block, key_block, preferred_element_type...  46.3 us
    all_gather x1, blocking collectives, shards(): lax.all_gather(w_out, 'dp', axis=1, tiled=True)  46 us
    all_gather x1, waiting for transfers between devices, shards(): lax.all_gather(w_down, 'dp', axis=1, tiled=True)  38.4 us
    reduce_scatter x1, waiting for transfers between devices, shards(): lax.psum_scatter(jnp.dot(context, full_out, preferred_element_type=jnp.fl...  32.7 us
    all_gather x1, blocking collectives, shards(): lax.all_gather(w_key, 'dp', axis=0, tiled=True)  31.2 us
    all_gather x1, blocking collectives, shards(): lax.all_gather(w_value, 'dp', axis=0, tiled=True)  31.2 us
    all_gather x1, blocking collectives, shards(): lax.all_gather(w_query, 'dp', axis=0, tiled=True)  31 us
  transfers between devices with their start and end apart: 18, of which 12 were waited for; matrix products, arithmetic and copies ran while one was open for 8% of the time, Pallas kernels for 0%

profile of v1, /device:TPU:0, one launch (start us, length us, event | category | flops | bytes accessed | tf_op | source)
XLA Modules:
  0.0 776.2 jit_solution(7014333604060535724)
XLA Ops:
  12.9 23.7 %all-reduce.5 = (bf16[768]{0:T(1024)(128)(2,1)S(1)}, bf16[768]{0:T(1024)(128)(2,1)}) all-reduce(bf16[768]{0:T(1024)(128)(2,1)S(1)} %dynamic-update-slice, bf16[768]{0:T(1024)(128)(2,1)S(1)} %dynamic-update-slice.1), channel_id=1, replica_groups=mesh['dp'=8,'tensor'=4] {'dp'}, use_global_device_ids=true, to_apply=%add.2 | all-reduce | flops 1536 | bytes 6144
  41.0 31.2 %all_gather.35 = bf16[768,192]{1,0:T(8,128)(2,1)S(1)} all-gather(bf16[96,192]{1,0:T(8,128)(2,1)} %param.22), channel_id=1, replica_groups=mesh['dp'=8,'tensor'=4] {'dp'}, dimensions={0}, use_global_device_ids=true | all-gather | bytes 331776 | tf_op jit(solution)/shard_map/all_gather | solution.py:78
  72.2 31.2 %all_gather.36 = bf16[768,192]{1,0:T(8,128)(2,1)S(1)} all-gather(bf16[96,192]{1,0:T(8,128)(2,1)} %param.23), channel_id=1, replica_groups=mesh['dp'=8,'tensor'=4] {'dp'}, dimensions={0}, use_global_device_ids=true | all-gather | bytes 331776 | tf_op jit(solution)/shard_map/all_gather | solution.py:79
  110.2 46.0 %all_gather.38 = bf16[192,768]{0,1:T(8,128)(2,1)} all-gather(bf16[192,96]{0,1:T(8,128)(2,1)S(1)} %copy.48), channel_id=1, replica_groups=mesh['dp'=8,'tensor'=4] {'dp'}, dimensions={1}, use_global_device_ids=true | all-gather | bytes 331776 | tf_op jit(solution)/shard_map/all_gather | solution.py:80
  156.2 31.0 %all_gather.37 = bf16[768,192]{1,0:T(8,128)(2,1)S(1)} all-gather(bf16[96,192]{1,0:T(8,128)(2,1)S(1)} %copy-done.36), channel_id=1, replica_groups=mesh['dp'=8,'tensor'=4] {'dp'}, dimensions={0}, use_global_device_ids=true | all-gather | bytes 331776 | tf_op jit(solution)/shard_map/all_gather | solution.py:77
  193.2 72.5 %while.29 = (s32[]{:T(128)}, bf16[2,640,192]{1,2,0:T(8,128)(2,1)}, f32[2,3,640]{2,1,0:T(4,128)S(1)}, s32[2]{0:T(128)S(1)}, bf16[2816,384]{0,1:T(8,128)(2,1)}, /*...) while((s32[]{:T(128)}, bf16[2,640,192]{1,2,0:T(8,128)(2,1)}, ...), condition=%wide.region_6.7_spmd.clone, body=%wide.region_3.6_spmd.clone.sunk | while | flops 1133730560 | bytes 66249560 | solution.py:163
  201.3 8.0 %fusion.136 = (f32[3,640]{1,0:T(4,128)S(1)}, f32[3,640,2176]{2,1,0:T(8,128)}) fusion(pred[640,2176]{1,0:T(8,128)(4,1)S(1)} %fusion.135, bf16[640,3,64]{0,2,1:T(8,128)(2,1)S(1)} %bitcast.149, bf16[2176,3,64]{0,2,1:T(8,128)(2,1)S(1)} %bitcast.146), kind=kOutput, calls=%fused_computation.7.clone.1 | convolution fusion | flops 547305600 | bytes 19193344 | tf_op jit(solution)/shard_map/while/body/eval_jaxpr/qhd,khd->hqk/dot_general | solution.py:146
  209.3 10.5 %fusion.137 = f32[3,640]{1,0:T(4,128)S(1)} fusion(f32[3,640,2176]{2,1,0:T(8,128)} %get-tuple-element.566, f32[3,640]{1,0:T(4,128)S(1)} %get-tuple-element.567, pred[640,2176]{1,0:T(8,128)(4,1)S(1)} %fusion.135), kind=kLoop, calls=%fused_computation.8.clone.1 | loop fusion | flops 16709760 | bytes 18119680 | tf_op jit(solution)/shard_map/while/body/eval_jaxpr/reduce_sum | solution.py:155
  219.8 8.8 %fusion.138 = bf16[3,64,640]{2,1,0:T(8,128)(2,1)S(1)} fusion(bf16[2176,3,64]{0,2,1:T(8,128)(2,1)S(1)} %bitcast.145, f32[3,640,2176]{2,1,0:T(8,128)} %get-tuple-element.566, f32[3,640]{1,0:T(4,128)S(1)} %fusion.137, f32[3,640]{1,0:T(4,128)S(1)} %get-tuple-element.567, pred[640,2176]{1,0:T(8,128)(4,1)S(1)} %fusion.135), kind=kOutput, calls=%fused_computation.15.clone.1 | convolution fusion | flops 555786240 | bytes 19201024 | tf_op jit(solution)/shard_map/while/body/eval_jaxpr/hqk,khd->qhd/dot_general | solution.py:157
  237.5 8.0 %fusion.136 = (f32[3,640]{1,0:T(4,128)S(1)}, f32[3,640,2176]{2,1,0:T(8,128)}) fusion(pred[640,2176]{1,0:T(8,128)(4,1)S(1)} %fusion.135, bf16[640,3,64]{0,2,1:T(8,128)(2,1)S(1)} %bitcast.149, bf16[2176,3,64]{0,2,1:T(8,128)(2,1)S(1)} %bitcast.146), kind=kOutput, calls=%fused_computation.7.clone.1 | convolution fusion | flops 547305600 | bytes 19193344 | tf_op jit(solution)/shard_map/while/body/eval_jaxpr/qhd,khd->hqk/dot_general | solution.py:146
  245.5 10.5 %fusion.137 = f32[3,640]{1,0:T(4,128)S(1)} fusion(f32[3,640,2176]{2,1,0:T(8,128)} %get-tuple-element.566, f32[3,640]{1,0:T(4,128)S(1)} %get-tuple-element.567, pred[640,2176]{1,0:T(8,128)(4,1)S(1)} %fusion.135), kind=kLoop, calls=%fused_computation.8.clone.1 | loop fusion | flops 16709760 | bytes 18119680 | tf_op jit(solution)/shard_map/while/body/eval_jaxpr/reduce_sum | solution.py:155
  256.0 8.9 %fusion.138 = bf16[3,64,640]{2,1,0:T(8,128)(2,1)S(1)} fusion(bf16[2176,3,64]{0,2,1:T(8,128)(2,1)S(1)} %bitcast.145, f32[3,640,2176]{2,1,0:T(8,128)} %get-tuple-element.566, f32[3,640]{1,0:T(4,128)S(1)} %fusion.137, f32[3,640]{1,0:T(4,128)S(1)} %get-tuple-element.567, pred[640,2176]{1,0:T(8,128)(4,1)S(1)} %fusion.135), kind=kOutput, calls=%fused_computation.15.clone.1 | convolution fusion | flops 555786240 | bytes 19201024 | tf_op jit(solution)/shard_map/while/body/eval_jaxpr/hqk,khd->qhd/dot_general | solution.py:157
  271.0 32.7 %reduce-scatter.5.cloned.1.call-done = bf16[320,768]{1,0:T(8,128)(2,1)} async-done(((bf16[1280,768]{1,0:T(8,128)(2,1)}), bf16[320,768]{1,0:T(8,128)(2,1)}) %reduce-scatter.5.cloned.1.call-update) | async-done | bytes 491536 | tf_op jit(solution)/shard_map/reduce_scatter | solution.py:165
  308.4 8.7 %all-gather.10.cloned.1.call-done = bf16[768,768]{1,0:T(8,128)(2,1)} async-done(((bf16[96,768]{1,0:T(8,128)(2,1)}), bf16[768,768]{1,0:T(8,128)(2,1)}) %all-gather.10.cloned.1.call-update) | async-done | bytes 1179664 | tf_op jit(solution)/shard_map/all_gather | solution.py:82
  317.1 22.3 %all-gather.8.cloned.1.call-done = bf16[1280,768]{1,0:T(8,128)(2,1)} async-done(((bf16[320,768]{1,0:T(8,128)(2,1)}), bf16[1280,768]{1,0:T(8,128)(2,1)}) %all-gather.8.cloned.1.call-update) | async-done | bytes 1966096 | tf_op jit(solution)/shard_map/all_gather | solution.py:174
  344.9 38.4 %all-gather.12.cloned.1.call-done = bf16[768,768]{0,1:T(8,128)(2,1)} async-done(((bf16[768,96]{0,1:T(8,128)(2,1)}), bf16[768,768]{0,1:T(8,128)(2,1)}) %all-gather.12.cloned.1.call-update) | async-done | bytes 1179664 | tf_op jit(solution)/shard_map/all_gather | solution.py:83
  383.3 21.9 %all-gather.14.cloned.1.call-done = bf16[1280,768]{1,0:T(8,128)(2,1)} async-done(((bf16[320,768]{1,0:T(8,128)(2,1)}), bf16[1280,768]{1,0:T(8,128)(2,1)}) %all-gather.14.cloned.1.call-update) | async-done | bytes 1966096 | tf_op jit(solution)/shard_map/all_gather | solution.py:184
  405.1 13.1 %add_convert_fusion = (bf16[1280,768]{1,0:T(8,128)(2,1)S(1)}, f32[1280,768]{1,0:T(8,128)}) fusion(f32[1280,768]{1,0:T(8,128)} %fusion.64, bf16[1280,768]{1,0:T(8,128)(2,1)} %all-gather.14.cloned.1.call-done, bf16[768,768]{0,1:T(8,128)(2,1)} %all-gather.12.cloned.1.call-done), kind=kOutput, calls=%fused_computation.47 | convolution fusion | flops 1580728320 | bytes 12976128 | tf_op jit(solution)/shard_map/td,fd->tf/dot_general | solution.py:186
  424.0 30.8 %reduce-scatter.9.cloned.1.call-done = bf16[320,768]{1,0:T(8,128)(2,1)} async-done(((bf16[1280,768]{1,0:T(8,128)(2,1)}), bf16[320,768]{1,0:T(8,128)(2,1)}) %reduce-scatter.9.cloned.1.call-update) | async-done | bytes 491536 | tf_op jit(solution)/shard_map/reduce_scatter | solution.py:194
  463.9 23.8 %all-to-all-done = bf16[4,320,768]{2,1,0:T(8,128)(2,1)S(1)} async-done(((bf16[4,320,768]{2,1,0:T(8,128)(2,1)}), bf16[4,320,768]{2,1,0:T(8,128)(2,1)S(1)}, u32[]{:S(2)}, u32[]{:S(2)}) %all-to-all-start) | async-done | bytes 1966112 | tf_op jit(solution)/shard_map/all_to_all | solution.py:207
  492.5 112.6 %while.30 = (s32[]{:T(128)}, bf16[1280,192]{0,1:T(8,128)(2,1)}, f32[2816,384]{0,1:T(8,128)}, bf16[2816,384]{0,1:T(8,128)(2,1)}, s32[2816]{0:T(1024)S(1)}, /*inde...) while((s32[]{:T(128)}, bf16[1280,192]{0,1:T(8,128)(2,1)}, ...), condition=%wide.region_14.15_spmd.clone, body=%wide.region_12.14_spmd.clone.sunk | while | flops 2727729920 | bytes 220916592 | solution.py:257
  500.2 8.1 %fusion.150 = f32[3,640,2176]{2,1,0:T(8,128)} fusion(bf16[640,3,64]{0,2,1:T(8,128)(2,1)S(1)} %bitcast.142, bf16[2176,3,64]{0,2,1:T(8,128)(2,1)S(1)} %bitcast.141), kind=kOutput, calls=%fused_computation.138.clone.1 | convolution fusion | flops 534773760 | bytes 17793024 | tf_op jit(solution)/shard_map/while/body/eval_jaxpr/qhd,khd->hqk/dot_general | solution.py:223
  508.3 15.1 %multiply_reduce_fusion.3 = (f32[3,640]{1,0:T(4,128)S(1)}, f32[3,640,2176]{2,1,0:T(8,128)}) fusion(f32[3,640,2176]{2,1,0:T(8,128)} %fusion.150, f32[3,640]{1,0:T(4,128)S(1)} %dynamic-slice_bitcast_fusion.2, bf16[640,3,64]{0,2,1:T(8,128)(2,1)S(1)} %bitcast.139, bf16[2176,3,64]{0,2,1:T(8,128)(2,1)S(1)} %bitcast.136, pred[640,2176]{1,0:T(8,128)(4,1)S(1)} %fusion.151), kind=kOutput, calls=%fused_computation.24.clone.1 | convolution fusion | flops 555661440 | bytes 35912704 | tf_op jit(solution)/shard_map/while/body/eval_jaxpr/qhd,khd->hqk/dot_general | solution.py:146
  523.4 11.4 %multiply_convert_fusion.4 = bf16[3,640,2176]{2,1,0:T(8,128)(2,1)S(1)} fusion(f32[3,640,2176]{2,1,0:T(8,128)} %get-tuple-element.583, f32[3,640,2176]{2,1,0:T(8,128)} %fusion.150, f32[3,640]{1,0:T(4,128)S(1)} %get-tuple-element.584), kind=kLoop, calls=%fused_computation.23.clone.1 | loop fusion | flops 12533760 | bytes 41786880 | tf_op jit(solution)/shard_map/while/body/eval_jaxpr/convert_element_type | solution.py:227
  556.5 8.1 %fusion.150 = f32[3,640,2176]{2,1,0:T(8,128)} fusion(bf16[640,3,64]{0,2,1:T(8,128)(2,1)S(1)} %bitcast.142, bf16[2176,3,64]{0,2,1:T(8,128)(2,1)S(1)} %bitcast.141), kind=kOutput, calls=%fused_computation.138.clone.1 | convolution fusion | flops 534773760 | bytes 17793024 | tf_op jit(solution)/shard_map/while/body/eval_jaxpr/qhd,khd->hqk/dot_general | solution.py:223
  564.5 15.1 %multiply_reduce_fusion.3 = (f32[3,640]{1,0:T(4,128)S(1)}, f32[3,640,2176]{2,1,0:T(8,128)}) fusion(f32[3,640,2176]{2,1,0:T(8,128)} %fusion.150, f32[3,640]{1,0:T(4,128)S(1)} %dynamic-slice_bitcast_fusion.2, bf16[640,3,64]{0,2,1:T(8,128)(2,1)S(1)} %bitcast.139, bf16[2176,3,64]{0,2,1:T(8,128)(2,1)S(1)} %bitcast.136, pred[640,2176]{1,0:T(8,128)(4,1)S(1)} %fusion.151), kind=kOutput, calls=%fused_computation.24.clone.1 | convolution fusion | flops 555661440 | bytes 35912704 | tf_op jit(solution)/shard_map/while/body/eval_jaxpr/qhd,khd->hqk/dot_general | solution.py:146
  579.7 11.4 %multiply_convert_fusion.4 = bf16[3,640,2176]{2,1,0:T(8,128)(2,1)S(1)} fusion(f32[3,640,2176]{2,1,0:T(8,128)} %get-tuple-element.583, f32[3,640,2176]{2,1,0:T(8,128)} %fusion.150, f32[3,640]{1,0:T(4,128)S(1)} %get-tuple-element.584), kind=kLoop, calls=%fused_computation.23.clone.1 | loop fusion | flops 12533760 | bytes 41786880 | tf_op jit(solution)/shard_map/while/body/eval_jaxpr/convert_element_type | solution.py:227
  611.3 26.8 %collective-permute-done.3 = bf16[256,384]{0,1:T(8,128)(2,1)S(1)} collective-permute-done((bf16[256,384]{0,1:T(8,128)(2,1)S(1)}, bf16[256,384]{0,1:T(8,128)(2,1)S(1)}, u32[]{:S(2)}, u32[]{:S(2)}) %collective-permute-start.3) | collective-permute-done | bytes 196640 | tf_op jit(solution)/shard_map/ppermute | solution.py:16
  671.4 10.9 %all-to-all-done.4 = bf16[8,768,96]{1,2,0:T(8,128)(2,1)} async-done(((bf16[8,768,96]{1,2,0:T(8,128)(2,1)}), bf16[8,768,96]{1,2,0:T(8,128)(2,1)}, u32[]{:S(2)}, u32[]{:S(2)}) %all-to-all-start.4) | async-done | bytes 1179680 | tf_op jit(solution)/shard_map/all_to_all | solution.py:27
  690.4 6.3 all-reduce.4
  714.3 15.6 %all-to-all-done.1 = bf16[8,96,577]{2,1,0:T(8,128)(2,1)S(1)} async-done(((bf16[8,96,577]{2,1,0:T(8,128)(2,1)}), bf16[8,96,577]{2,1,0:T(8,128)(2,1)S(1)}, u32[]{:S(2)}, u32[]{:S(2)}) %all-to-all-start.1) | async-done | bytes 886304 | tf_op jit(solution)/shard_map/all_to_all | solution.py:27
  742.9 24.3 %all-to-all-done.3 = bf16[8,96,769]{2,1,0:T(8,128)(2,1)S(1)} async-done(((bf16[8,96,769]{2,1,0:T(8,128)(2,1)}), bf16[8,96,769]{2,1,0:T(8,128)(2,1)S(1)}, u32[]{:S(2)}, u32[]{:S(2)}) %all-to-all-start.3) | async-done | bytes 1181216 | tf_op jit(solution)/shard_map/all_to_all | solution.py:27
  (260 shorter events, 195.1 us)
Async XLA Ops:
  8.0 95.4 %all-gather.6.cloned.1.call-start = ((), (), s32[]{:S(2)}) async-start(), calls=%async_computation.9 | async-start | bytes 2457600 | tf_op jit(solution)/shard_map/all_gather | solution.py:101
  9.3 30.9 %copy-start.37 = (f32[320]{0:T(512)}, f32[320]{0:T(512)S(1)}, u32[]{:S(2)}) copy-start(f32[320]{0:T(512)S(1)} %add_rsqrt_fusion.1) | copy-start | bytes 3844
  39.2 264.5 %reduce-scatter.5.cloned.1.call-start = ((), (), s32[]{:S(2)}) async-start(), calls=%async_computation.10 | async-start | bytes 2457600 | tf_op jit(solution)/shard_map/reduce_scatter | solution.py:165
  72.2 36.3 %copy-start.20 = (bf16[768,192]{1,0:T(8,128)(2,1)}, bf16[768,192]{1,0:T(8,128)(2,1)S(1)}, u32[]{:S(2)}) copy-start(bf16[768,192]{1,0:T(8,128)(2,1)S(1)} %all_gather.35) | copy-start | bytes 884740
  103.4 52.9 %copy-start.22 = (bf16[768,192]{1,0:T(8,128)(2,1)}, bf16[768,192]{1,0:T(8,128)(2,1)S(1)}, u32[]{:S(2)}) copy-start(bf16[768,192]{1,0:T(8,128)(2,1)S(1)} %all_gather.36) | copy-start | bytes 884740
  103.4 52.9 %copy-start.36 = (bf16[96,192]{1,0:T(8,128)(2,1)S(1)}, bf16[96,192]{1,0:T(8,128)(2,1)}, u32[]{:S(2)}) copy-start(bf16[96,192]{1,0:T(8,128)(2,1)} %param.21) | copy-start | bytes 110596
  105.9 82.6 %copy-start.3 = (bf16[1280,768]{1,0:T(8,128)(2,1)S(1)}, bf16[1280,768]{1,0:T(8,128)(2,1)}, u32[]{:S(2)}) copy-start(bf16[1280,768]{1,0:T(8,128)(2,1)} %all-gather.6.cloned.1.call-done) | copy-start | bytes 5898244
  108.5 83.2 %collective-permute-start.1 = (bf16[1280,384]{0,1:T(8,128)(2,1)S(1)}, bf16[1280,384]{0,1:T(8,128)(2,1)S(1)}, u32[]{:S(2)}, u32[]{:S(2)}) collective-permute-start(bf16[1280,384]{0,1:T(8,128)(2,1)S(1)} %pad_maximum_fusion.1), channel_id=1, source_target_pairs={{0,4},{4,8},{8,12},{12,16},{16,20},{20,24},{24,28},{1,5},{5,9},{9,... | collective-permute-start | bytes 2949128 | tf_op jit(solution)/shard_map/ppermute | solution.py:16
  187.2 4.5 collective-permute-start
  265.7 38.0 %copy-start.1 = (bf16[320,768]{1,0:T(8,128)(2,1)S(1)}, bf16[320,768]{1,0:T(8,128)(2,1)}, u32[]{:S(2)}) copy-start(bf16[320,768]{1,0:T(8,128)(2,1)} %param.16) | copy-start | bytes 1474564
  266.9 40.2 %copy-start.11 = (bf16[2,24,8,640]{3,2,0,1:T(8,128)(2,1)}, bf16[2,24,8,640]{3,2,0,1:T(8,128)(2,1)S(1)}, u32[]{:S(2)}) copy-start(bf16[2,24,8,640]{3,2,0,1:T(8,128)(2,1)S(1)} %copy.67) | copy-start | bytes 1474564
  270.1 47.0 %all-gather.10.cloned.1.call-start = ((), (), s32[]{:S(2)}) async-start(), calls=%async_computation.12 | async-start | bytes 1327104 | tf_op jit(solution)/shard_map/all_gather | solution.py:82
  270.7 68.7 %all-gather.8.cloned.1.call-start = ((), (), s32[]{:S(2)}) async-start(), calls=%async_computation.11 | async-start | bytes 2457600 | tf_op jit(solution)/shard_map/all_gather | solution.py:174
  271.0 186.0 %copy-start.30 = (f32[768]{0:T(1024)}, f32[768]{0:T(1024)S(1)}, u32[]{:S(2)}) copy-start(f32[768]{0:T(1024)S(1)} %convert_element_type.159) | copy-start | bytes 9220
  305.0 152.0 %copy-start.34 = (f32[320]{0:T(512)}, f32[320]{0:T(512)S(1)}, u32[]{:S(2)}) copy-start(f32[320]{0:T(512)S(1)} %add_rsqrt_fusion) | copy-start | bytes 3844
  307.1 76.2 %all-gather.12.cloned.1.call-start = ((), (), s32[]{:S(2)}) async-start(), calls=%async_computation.13 | async-start | bytes 1327104 | tf_op jit(solution)/shard_map/all_gather | solution.py:83
  307.6 97.5 %all-gather.14.cloned.1.call-start = ((), (), s32[]{:S(2)}) async-start(), calls=%async_computation.15 | async-start | bytes 2457600 | tf_op jit(solution)/shard_map/all_gather | solution.py:184
  308.4 146.4 %reduce-scatter.9.cloned.1.call-start = ((), (), s32[]{:S(2)}) async-start(), calls=%async_computation.16 | async-start | bytes 2457600 | tf_op jit(solution)/shard_map/reduce_scatter | solution.py:194
  419.6 35.2 %copy-start.6 = (bf16[320,768]{1,0:T(8,128)(2,1)S(1)}, bf16[320,768]{1,0:T(8,128)(2,1)}, u32[]{:S(2)}) copy-start(bf16[320,768]{1,0:T(8,128)(2,1)} %reduce-scatter.5.cloned.1.call-done) | copy-start | bytes 1474564
  419.6 37.4 %copy-start.8 = (bf16[320,768]{1,0:T(8,128)(2,1)S(1)}, bf16[320,768]{1,0:T(8,128)(2,1)}, u32[]{:S(2)}) copy-start(bf16[320,768]{1,0:T(8,128)(2,1)} %param.17) | copy-start | bytes 1474564
  457.0 30.8 %copy-start.26 = (bf16[192,768]{0,1:T(8,128)(2,1)S(1)}, bf16[192,768]{0,1:T(8,128)(2,1)}, u32[]{:S(2)}) copy-start(bf16[192,768]{0,1:T(8,128)(2,1)} %all_gather.38) | copy-start | bytes 884740
  459.9 27.9 %all-to-all-start = ((bf16[4,320,768]{2,1,0:T(8,128)(2,1)}), bf16[4,320,768]{2,1,0:T(8,128)(2,1)S(1)}, u32[]{:S(2)}, u32[]{:S(2)}) async-start(bf16[4,320,768]{2,1,0:T(8,128)(2,1)} %stack.2), calls=%async_computation.3 | async-start | bytes 3932160 | tf_op jit(solution)/shard_map/all_to_all | solution.py:207
  463.5 225.3 %reduce-scatter.11.cloned.1.call-start = ((), (), s32[]{:S(2)}) async-start(), calls=%async_computation.17 | async-start | bytes 2457600 | tf_op jit(solution)/shard_map/reduce_scatter | solution.py:282
  607.7 30.3 %collective-permute-start.2 = (bf16[1280,384]{0,1:T(8,128)(2,1)S(1)}, bf16[1280,384]{0,1:T(8,128)(2,1)S(1)}, u32[]{:S(2)}, u32[]{:S(2)}) collective-permute-start(bf16[1280,384]{0,1:T(8,128)(2,1)S(1)} %slice.58), channel_id=1, source_target_pairs={{4,0},{8,4},{12,8},{16,12},{20,16},{24,20},{28,24},{5,1},{9,5},{13... | collective-permute-start | bytes 2949128 | tf_op jit(solution)/shard_map/ppermute | solution.py:16
  609.2 28.8 %collective-permute-start.3 = (bf16[256,384]{0,1:T(8,128)(2,1)S(1)}, bf16[256,384]{0,1:T(8,128)(2,1)S(1)}, u32[]{:S(2)}, u32[]{:S(2)}) collective-permute-start(bf16[256,384]{0,1:T(8,128)(2,1)S(1)} %slice.59), channel_id=1, source_target_pairs={{8,0},{12,4},{16,8},{20,12},{24,16},{28,20},{9,1},{13,5},{17,9},{2... | collective-permute-start | bytes 589832 | tf_op jit(solution)/shard_map/ppermute | solution.py:16
  610.5 29.3 %copy-start.21 = (bf16[768,192]{1,0:T(8,128)(2,1)S(1)}, bf16[768,192]{1,0:T(8,128)(2,1)}, u32[]{:S(2)}) copy-start(bf16[768,192]{1,0:T(8,128)(2,1)} %copy-done.20) | copy-start | bytes 884740
  650.1 32.2 %all-to-all-start.4 = ((bf16[8,768,96]{1,2,0:T(8,128)(2,1)}), bf16[8,768,96]{1,2,0:T(8,128)(2,1)}, u32[]{:S(2)}, u32[]{:S(2)}) async-start(bf16[8,768,96]{1,2,0:T(8,128)(2,1)} %bitcast.157), calls=%async_computation.8 | async-start | bytes 2359296 | tf_op jit(solution)/shard_map/all_to_all | solution.py:27
  654.3 84.0 %reduce-scatter.7.cloned.1.call-start = ((), (), s32[]{:S(2)}) async-start(), calls=%async_computation.14 | async-start | bytes 2457600 | tf_op jit(solution)/shard_map/reduce_scatter | solution.py:177
  682.3 17.5 %all-to-all-start.2 = ((bf16[8,192,96]{2,1,0:T(8,128)(2,1)}), bf16[8,192,96]{2,1,0:T(8,128)(2,1)}, u32[]{:S(2)}, u32[]{:S(2)}) async-start(bf16[8,192,96]{2,1,0:T(8,128)(2,1)} %bitcast.153), calls=%async_computation.6 | async-start | bytes 786432 | tf_op jit(solution)/shard_map/all_to_all | solution.py:27
  699.8 30.1 %all-to-all-start.1 = ((bf16[8,96,577]{2,1,0:T(8,128)(2,1)}), bf16[8,96,577]{2,1,0:T(8,128)(2,1)S(1)}, u32[]{:S(2)}, u32[]{:S(2)}) async-start(bf16[8,96,577]{2,1,0:T(8,128)(2,1)} %pad_maximum_fusion.2), calls=%async_computation.5 | async-start | bytes 1966080 | tf_op jit(solution)/shard_map/all_to_all | solution.py:27
  710.9 27.5 %copy-start.35 = (f32[320]{0:T(512)S(1)}, f32[320]{0:T(512)}, u32[]{:S(2)}) copy-start(f32[320]{0:T(512)} %copy-done.34) | copy-start | bytes 3844
  730.8 36.4 %all-to-all-start.3 = ((bf16[8,96,769]{2,1,0:T(8,128)(2,1)}), bf16[8,96,769]{2,1,0:T(8,128)(2,1)S(1)}, u32[]{:S(2)}, u32[]{:S(2)}) async-start(bf16[8,96,769]{2,1,0:T(8,128)(2,1)} %pad_maximum_fusion), calls=%async_computation.7 | async-start | bytes 2752512 | tf_op jit(solution)/shard_map/all_to_all | solution.py:27
  (37 other events, 373.4 us)
Sparse Core Ops, SparseCore 0:
  39.3 19.0 all-gather.5
  270.2 33.4 reduce-scatter.4
  424.1 30.6 reduce-scatter.8
Sparse Core Ops, SparseCore 1:
  272.8 44.3 all-gather.9
  319.2 20.1 all-gather.7
  341.7 41.5 all-gather.11
  384.9 20.1 all-gather.13
  643.3 28.8 reduce-scatter.10
  674.9 30.8 reduce-scatter.6
